TPU v7x, 32 devices: a whole 2x2x4 slice. The times are simulated.
32 devices in a mesh: ctx: 8 (over y, x, core), head: 4 (over z).
Axes of the slice: x: 2, y: 2, z: 4, core: 2. Of those that a mesh axis runs over, the one named last changes fastest.
Arguments:
- queries: bfloat16 [640, 8192], P(('ctx', 'head')), may hold values from -18 to 18
- keys: bfloat16 [640, 1024], P(('ctx', 'head')), may hold values from -4.5 to 4.5
- values: bfloat16 [640, 1024], P(('ctx', 'head')), may hold values from -12 to 12
- block_order: int32 [16], replicated, may hold values from 0 to 15, each once
Outputs:
- attended: bfloat16 [640, 8192], P(('ctx', 'head'))
Inputs may be any that keep to these rules, and one draw needn't show every extreme that they name: Storage block b holds sequence block block_order[b], its tokens in order; block_order is a permutation.
All inputs are finite; a program needn't handle non-finite values.
Results may differ from a plain program's by a relative error of at most 0.0049.
Values may be sent and summed in bfloat16 or wider, within the bound.
A program may use at most 64 MiB of HBM per device.

v0:
```python
import math

import jax
import jax.numpy as jnp
import numpy as np
from jax import lax
from jax.sharding import PartitionSpec as P

QUERY_HEADS = 64
VALUE_KEY_HEADS = 8
HEAD_DIMENSION = 128


def token_positions(block_order, row_ids, block_rows):
    block_ids = row_ids // block_rows
    block_table = jnp.arange(block_order.shape[0], dtype=jnp.int32)
    chosen = jnp.sum(
        jnp.where(block_ids[:, None] == block_table[None, :], block_order[None, :], 0), axis=1
    )
    return chosen * block_rows + row_ids % block_rows


def attend(states, query_block, query_pos, key_rows, value_rows, key_pos, key_heads, score_scale):
    max_old, total_old, weighted_old = states
    query_count = query_block.shape[0]
    head_size = key_rows.shape[1] // key_heads
    heads_per_group = query_block.shape[1] // (key_heads * head_size)
    head_total = key_heads * heads_per_group
    query_split = query_block.reshape(query_count, key_heads, heads_per_group, head_size)
    key_split = key_rows.reshape(-1, key_heads, head_size)
    value_split = value_rows.reshape(-1, key_heads, head_size)
    scores = (
        jnp.einsum("qkgd,nkd->kgqn", query_split, key_split, preferred_element_type=jnp.float32)
        * score_scale
    )
    visible = key_pos[None, :] <= query_pos[:, None]
    scores = jnp.where(visible[None, None], scores, -jnp.inf)
    max_prev = max_old.reshape(key_heads, heads_per_group, query_count)
    max_new = jnp.maximum(max_prev, jnp.max(scores, axis=3))
    weights = jnp.exp(scores - max_new[..., None])
    rescale = jnp.exp(max_prev - max_new)
    total_new = total_old.reshape(key_heads, heads_per_group, query_count) * rescale + jnp.sum(
        weights, axis=3
    )
    mixed_values = jnp.einsum(
        "kgqn,nkd->qkgd",
        weights.astype(jnp.bfloat16),
        value_split,
        preferred_element_type=jnp.float32,
    )
    weighted_new = (
        weighted_old.reshape(query_count, key_heads, heads_per_group, head_size)
        * jnp.transpose(rescale, (2, 0, 1))[..., None]
        + mixed_values
    )
    return (
        max_new.reshape(head_total, query_count),
        total_new.reshape(head_total, query_count),
        weighted_new.reshape(query_count, head_total * head_size),
    )


def on_device(queries, keys, values, block_order):
    head_count = lax.axis_size("head")
    ctx_index = lax.axis_index("ctx")
    tokens_per_shard = queries.shape[0]
    query_heads = QUERY_HEADS // head_count
    heads_per_group = QUERY_HEADS // VALUE_KEY_HEADS
    local_kv = max(1, query_heads // heads_per_group)
    score_scale = HEAD_DIMENSION ** (-0.5)
    placement_index = np.array(
        [
            slot_number * query_heads // heads_per_group + offset
            for slot_number in range(head_count)
            for offset in range(local_kv)
        ],
        dtype=np.int32,
    )
    key_placements = keys.reshape(tokens_per_shard, VALUE_KEY_HEADS, HEAD_DIMENSION)[
        :, placement_index, :
    ].reshape(tokens_per_shard, head_count * local_kv * HEAD_DIMENSION)
    value_placements = values.reshape(tokens_per_shard, VALUE_KEY_HEADS, HEAD_DIMENSION)[
        :, placement_index, :
    ].reshape(tokens_per_shard, head_count * local_kv * HEAD_DIMENSION)
    tok_ctx = tokens_per_shard * head_count
    block_rows = tok_ctx // 2
    query_pos = token_positions(
        block_order, ctx_index * tok_ctx + jnp.arange(tok_ctx, dtype=jnp.int32), block_rows
    )

    def make_fold(query_all, key_heads, position_of):

        def tile(states, key_rows, value_rows, key_pos):
            updated = []
            for number in range(2):
                query_block = query_all[number * block_rows : (number + 1) * block_rows]
                block_pos = query_pos[number * block_rows : (number + 1) * block_rows]
                reach = jnp.min(key_pos) <= jnp.max(block_pos)
                updated.append(
                    lax.cond(
                        reach,
                        lambda carry_state: attend(
                            carry_state,
                            query_block,
                            block_pos,
                            key_rows,
                            value_rows,
                            key_pos,
                            key_heads,
                            score_scale,
                        ),
                        lambda carry_state: carry_state,
                        states[number],
                    )
                )
            return tuple(updated)

        def fold_step(states, key_piece, first_row):
            key_rows, value_rows = key_piece
            count = key_rows.shape[0]
            key_pos = position_of(jnp.arange(count, dtype=jnp.int32))
            piece_rows = tok_ctx * math.gcd(count // tok_ctx, 4)
            splits = count // piece_rows

            def scan_step(carry_states, parts):
                return (tile(carry_states, parts[0], parts[1], parts[2]), None)

            states, unused = lax.scan(
                scan_step,
                states,
                (
                    key_rows.reshape(splits, piece_rows, -1),
                    value_rows.reshape(splits, piece_rows, -1),
                    key_pos.reshape(splits, piece_rows),
                ),
            )
            return states

        return fold_step

    local_q, local_k, local_v = (
        lax.all_to_all(queries, "head", split_axis=1, concat_axis=0, tiled=True),
        lax.all_to_all(key_placements, "head", split_axis=1, concat_axis=0, tiled=True),
        lax.all_to_all(value_placements, "head", split_axis=1, concat_axis=0, tiled=True),
    )

    def full_positions(row_ids):
        return token_positions(block_order, row_ids, block_rows)

    fold_each = make_fold(local_q, local_kv, full_positions)
    one_state = (
        jnp.full((query_heads, block_rows), -1e30, jnp.float32),
        jnp.zeros((query_heads, block_rows), jnp.float32),
        jnp.zeros((block_rows, query_heads * HEAD_DIMENSION), jnp.float32),
    )
    states = fold_each(
        (one_state, one_state),
        (
            lax.all_gather(local_k, "ctx", axis=0, tiled=True),
            lax.all_gather(local_v, "ctx", axis=0, tiled=True),
        ),
        jnp.int32(0),
    )
    total_all = jnp.concatenate([states[0][1], states[1][1]], axis=1)
    weighted_all = jnp.concatenate([states[0][2], states[1][2]], axis=0)
    weighted_all = weighted_all.reshape(tok_ctx, query_heads, HEAD_DIMENSION)
    attended = (
        (weighted_all / total_all.T[:, :, None])
        .reshape(tok_ctx, query_heads * HEAD_DIMENSION)
        .astype(jnp.bfloat16)
    )
    return lax.all_to_all(attended, "head", split_axis=0, concat_axis=1, tiled=True)


def solution(mesh):
    placed = (P(("ctx", "head"), None), P(("ctx", "head"), None), P(("ctx", "head"), None), P())
    return jax.shard_map(
        on_device, mesh=mesh, in_specs=placed, out_specs=P(("ctx", "head"), None), check_vma=False
    )
```

profile of v0, /device:TPU:0, one launch (start us, length us, event | category | flops | bytes accessed | tf_op | source)
XLA Modules:
  0.0 79.5 jit_solution(4097366755005367312)
XLA Ops:
  0.0 0.8 %copy.104 = bf16[3,8,8,128]{3,2,1,0:T(8,128)(2,1)S(1)} copy(bf16[3,8,8,128]{3,1,2,0:T(8,128)(2,1)} %bitcast.127) | data formatting | bytes 98304
  0.9 0.6 gather_fusion
  1.5 0.6 copy.79
  2.1 6.4 %all-to-all-start = ((bf16[20,4,256]{2,0,1:T(8,128)(2,1)}), bf16[20,4,256]{2,0,1:T(8,128)(2,1)S(1)}, u32[]{:S(2)}, u32[]{:S(2)}) async-start(bf16[20,4,256]{2,0,1:T(8,128)(2,1)} %copy.79), calls=%async_computation | async-start | bytes 98304 | tf_op jit(solution)/shard_map/all_to_all | solution.py:143
  8.6 0.1 select_reduce_fusion
  8.8 0.6 gather_fusion.1
  9.4 0.6 copy.82
  10.0 0.2 all_to_all.62
  10.2 0.9 %copy.83 = bf16[20,4,2048]{2,0,1:T(8,128)(2,1)} copy(bf16[20,4,2048]{2,1,0:T(4,128)(2,1)S(1)} %all_to_all.62) | data formatting | bytes 655360 | tf_op jit(solution)/shard_map/all_to_all | solution.py:142
  11.2 3.1 %all-to-all-done = bf16[20,4,256]{2,0,1:T(8,128)(2,1)S(1)} async-done(((bf16[20,4,256]{2,0,1:T(8,128)(2,1)}), bf16[20,4,256]{2,0,1:T(8,128)(2,1)S(1)}, u32[]{:S(2)}, u32[]{:S(2)}) %all-to-all-start) | async-done | bytes 40992 | tf_op jit(solution)/shard_map/all_to_all | solution.py:143
  14.3 3.3 %all-to-all-start.1 = ((bf16[20,4,256]{2,0,1:T(8,128)(2,1)}), bf16[20,4,256]{2,0,1:T(8,128)(2,1)S(1)}, u32[]{:S(2)}, u32[]{:S(2)}) async-start(bf16[20,4,256]{2,0,1:T(8,128)(2,1)} %copy.82), calls=%async_computation.1 | async-start | bytes 98304 | tf_op jit(solution)/shard_map/all_to_all | solution.py:144
  17.6 0.1 select_reduce_fusion.1
  17.7 5.6 %all-to-all-done.1 = bf16[20,4,256]{2,0,1:T(8,128)(2,1)S(1)} async-done(((bf16[20,4,256]{2,0,1:T(8,128)(2,1)}), bf16[20,4,256]{2,0,1:T(8,128)(2,1)S(1)}, u32[]{:S(2)}, u32[]{:S(2)}) %all-to-all-start.1) | async-done | bytes 40992 | tf_op jit(solution)/shard_map/all_to_all | solution.py:144
  23.2 3.5 %all-to-all-start.2 = ((bf16[20,4,2048]{2,0,1:T(8,128)(2,1)}), bf16[20,4,2048]{2,0,1:T(8,128)(2,1)S(1)}, u32[]{:S(2)}, u32[]{:S(2)}) async-start(bf16[20,4,2048]{2,0,1:T(8,128)(2,1)} %copy.83), calls=%async_computation.2 | async-start | bytes 786432 | tf_op jit(solution)/shard_map/all_to_all | solution.py:142
  26.8 0.8 slice_reduce_fusion
  27.6 9.5 %all_gather.6 = bf16[640,256]{1,0:T(8,128)(2,1)S(1)} all-gather(bf16[80,256]{1,0:T(8,128)(2,1)S(1)} %all_to_all.57), channel_id=1, replica_groups=mesh['ctx'=8,'head'=4] {'ctx'}, dimensions={0}, use_global_device_ids=true | all-gather | bytes 368640 | tf_op jit(solution)/shard_map/all_gather | solution.py:159
  37.1 9.4 %all_gather.7 = bf16[640,256]{1,0:T(8,128)(2,1)S(1)} all-gather(bf16[80,256]{1,0:T(8,128)(2,1)S(1)} %all_to_all.61), channel_id=1, replica_groups=mesh['ctx'=8,'head'=4] {'ctx'}, dimensions={0}, use_global_device_ids=true | all-gather | bytes 368640 | tf_op jit(solution)/shard_map/all_gather | solution.py:160
  46.7 13.6 %while.21 = (s32[]{:T(128)}, f32[16,40]{1,0:T(8,128)S(1)}, f32[16,40]{1,0:T(8,128)S(1)}, f32[40,2048]{1,0:T(8,128)S(1)}, f32[16,40]{1,0:T(8,128)S(1)}, /*index=5...) while((s32[]{:T(128)}, f32[16,40]{1,0:T(8,128)S(1)}, ...), condition=%wide.region_14.15_spmd, body=%wide.region_4.14_spmd.sunk | while | flops 212941120 | bytes 14552109 | solution.py:128
  46.7 0.6 fusion.35
  48.6 1.7 %conditional.4 = ((f32[16,40]{1,0:T(8,128)S(1)}, f32[16,40]{1,0:T(8,128)S(1)}, f32[40,2048]{1,0:T(8,128)S(1)})) conditional(s32[]{:T(128)} %convert_element_type.26, (f32[16,40]{1,0:T(8,128)S(1)}, f32[16,40]{1,0:T(8,128)S(1)}, f32[40,2048]{1,0:T(8,128)S(1)}) %tuple.53, (s32[320]{0:T(512)S(1)}, s32[80]{0:T(128)S(1)}, bf16[320,256]{1,0:T(8,128)(2,1)S(1)}, ...), branch_computations={%region_6.6_spmd, %region_7.9_spmd} | conditional | flops 106470400 | bytes 6946752 | solution.py:100
  48.8 0.4 fusion.32
  49.2 0.3 fusion.4
  49.7 0.4 fusion.2
  50.2 0.1 copy.135
  51.7 1.8 %conditional.5 = ((f32[16,40]{1,0:T(8,128)S(1)}, f32[16,40]{1,0:T(8,128)S(1)}, f32[40,2048]{1,0:T(8,128)S(1)})) conditional(s32[]{:T(128)} %convert_element_type.27, (f32[16,40]{1,0:T(8,128)S(1)}, f32[16,40]{1,0:T(8,128)S(1)}, f32[40,2048]{1,0:T(8,128)S(1)}) %tuple.55, (s32[320]{0:T(512)S(1)}, s32[80]{0:T(128)S(1)}, ...), branch_computations={%region_10.10_spmd, %region_11.13_spmd} | conditional | flops 106470400 | bytes 6947072 | solution.py:100
  52.0 0.4 fusion.33
  52.4 0.3 fusion.16
  52.9 0.4 fusion.14
  53.4 0.1 copy.136
  53.5 0.6 fusion.35
  55.4 1.7 %conditional.4 = ((f32[16,40]{1,0:T(8,128)S(1)}, f32[16,40]{1,0:T(8,128)S(1)}, f32[40,2048]{1,0:T(8,128)S(1)})) conditional(s32[]{:T(128)} %convert_element_type.26, (f32[16,40]{1,0:T(8,128)S(1)}, f32[16,40]{1,0:T(8,128)S(1)}, f32[40,2048]{1,0:T(8,128)S(1)}) %tuple.53, (s32[320]{0:T(512)S(1)}, s32[80]{0:T(128)S(1)}, bf16[320,256]{1,0:T(8,128)(2,1)S(1)}, ...), branch_computations={%region_6.6_spmd, %region_7.9_spmd} | conditional | flops 106470400 | bytes 6946752 | solution.py:100
  55.6 0.4 fusion.32
  56.0 0.3 fusion.4
  56.5 0.4 fusion.2
  57.0 0.1 copy.135
  58.5 1.8 %conditional.5 = ((f32[16,40]{1,0:T(8,128)S(1)}, f32[16,40]{1,0:T(8,128)S(1)}, f32[40,2048]{1,0:T(8,128)S(1)})) conditional(s32[]{:T(128)} %convert_element_type.27, (f32[16,40]{1,0:T(8,128)S(1)}, f32[16,40]{1,0:T(8,128)S(1)}, f32[40,2048]{1,0:T(8,128)S(1)}) %tuple.55, (s32[320]{0:T(512)S(1)}, s32[80]{0:T(128)S(1)}, ...), branch_computations={%region_10.10_spmd, %region_11.13_spmd} | conditional | flops 106470400 | bytes 6947072 | solution.py:100
  58.7 0.4 fusion.33
  59.2 0.3 fusion.16
  59.7 0.4 fusion.14
  60.2 0.1 copy.136
  60.5 0.1 copy.84
  60.6 0.2 div.34
  60.8 0.1 div.35
  60.9 0.1 divide_convert_fusion
  61.0 17.0 %all_to_all.73 = bf16[4,20,2048]{2,1,0:T(8,128)(2,1)S(1)} all-to-all(bf16[4,20,2048]{2,1,0:T(8,128)(2,1)S(1)} %divide_convert_fusion), channel_id=1, replica_groups=mesh['ctx'=8,'head'=4] {'head'}, dimensions={0} | all-to-all | bytes 655360 | tf_op jit(solution)/shard_map/all_to_all | solution.py:172
  78.1 0.3 copy.85
  78.4 0.2 pad.6
  78.5 1.0 %copy.106 = bf16[3,8,4,2048]{3,1,2,0:T(8,128)(2,1)} copy(bf16[3,8,4,2048]{3,2,1,0:T(4,128)(2,1)S(1)} %bitcast.118) | data formatting | bytes 786432
  (76 shorter events, 2.2 us)
Async XLA Ops:
  1.5 7.1 %copy-start.2 = (s32[16]{0:T(128)S(1)}, s32[16]{0:T(128)}, u32[]{:S(2)}) copy-start(s32[16]{0:T(128)} %param.16) | copy-start | bytes 196
  1.5 7.2 %copy-start.1 = (bf16[20,1024]{1,0:T(8,128)(2,1)S(1)}, bf16[20,1024]{1,0:T(8,128)(2,1)}, u32[]{:S(2)}) copy-start(bf16[20,1024]{1,0:T(8,128)(2,1)} %param.15) | copy-start | bytes 122884
  2.1 7.9 %copy-start = (bf16[20,8192]{1,0:T(8,128)(2,1)S(1)}, bf16[20,8192]{1,0:T(8,128)(2,1)}, u32[]{:S(2)}) copy-start(bf16[20,8192]{1,0:T(8,128)(2,1)} %param.13) | copy-start | bytes 983044
  2.1 12.2 %all-to-all-start = ((bf16[20,4,256]{2,0,1:T(8,128)(2,1)}), bf16[20,4,256]{2,0,1:T(8,128)(2,1)S(1)}, u32[]{:S(2)}, u32[]{:S(2)}) async-start(bf16[20,4,256]{2,0,1:T(8,128)(2,1)} %copy.79), calls=%async_computation | async-start | bytes 98304 | tf_op jit(solution)/shard_map/all_to_all | solution.py:143
  14.3 8.9 %all-to-all-start.1 = ((bf16[20,4,256]{2,0,1:T(8,128)(2,1)}), bf16[20,4,256]{2,0,1:T(8,128)(2,1)S(1)}, u32[]{:S(2)}, u32[]{:S(2)}) async-start(bf16[20,4,256]{2,0,1:T(8,128)(2,1)} %copy.82), calls=%async_computation.1 | async-start | bytes 98304 | tf_op jit(solution)/shard_map/all_to_all | solution.py:144
  23.2 23.3 %all-to-all-start.2 = ((bf16[20,4,2048]{2,0,1:T(8,128)(2,1)}), bf16[20,4,2048]{2,0,1:T(8,128)(2,1)S(1)}, u32[]{:S(2)}, u32[]{:S(2)}) async-start(bf16[20,4,2048]{2,0,1:T(8,128)(2,1)} %copy.83), calls=%async_computation.2 | async-start | bytes 786432 | tf_op jit(solution)/shard_map/all_to_all | solution.py:142
where the time goes:
time: 80.1 us; the launch traced here: 79.5 us
  blocking collectives  35.9 us (45%)
  starting transfers between devices  13.2 us (16%)
  waiting for transfers between devices  8.68 us (11%)
  local copies, waits for them, and re-layouts  8.23 us (10%)
  loops' own time  5.57 us (7%)
  other arithmetic  4.32 us (5%)
  matrix products  3.31 us (4%)
    all_to_all x1, blocking collectives, on_device(): lax.all_to_all(attended, 'head', split_axis=0, concat_axis=1, tiled=True)  17 us
    all_gather x1, blocking collectives, on_device(): lax.all_gather(local_k, 'ctx', axis=0, tiled=True)  9.46 us
    all_gather x1, blocking collectives, on_device(): lax.all_gather(local_v, 'ctx', axis=0, tiled=True)  9.41 us
    all_to_all x1, starting transfers between devices, on_device(): lax.all_to_all(key_placements, 'head', split_axis=1, concat_axis=0, tiled...  6.45 us
    all_to_all x1, waiting for transfers between devices, on_device(): lax.all_to_all(value_placements, 'head', split_axis=1, concat_axis=0, til...  5.58 us
    another operation x1, loops' own time, fold_step(): lax.scan(scan_step, states, (key_rows.reshape(splits, piece_rows, -1), va...  5.19 us
    all_to_all x1, starting transfers between devices, on_device(): lax.all_to_all(queries, 'head', split_axis=1, concat_axis=0, tiled=True)  3.46 us
    all_to_all x1, starting transfers between devices, on_device(): lax.all_to_all(value_placements, 'head', split_axis=1, concat_axis=0, til...  3.27 us
  transfers between devices with their start and end apart: 3, of which 2 were waited for; matrix products, arithmetic and copies ran while one was open for 4% of the time, Pallas kernels for 0%

commit v1 on v0

--- a/solution.py
+++ b/solution.py
@@ -1,9 +1,12 @@
+import functools
 import math
 
 import jax
 import jax.numpy as jnp
 import numpy as np
 from jax import lax
+from jax.experimental import pallas as pl
+from jax.experimental.pallas import tpu as pltpu
 from jax.sharding import PartitionSpec as P
 
 QUERY_HEADS = 64
@@ -172,8 +175,278 @@
     return lax.all_to_all(attended, "head", split_axis=0, concat_axis=1, tiled=True)
 
 
+ROWS = 20
+MAIN = 16
+REST = ROWS - MAIN
+GROUP = QUERY_HEADS // VALUE_KEY_HEADS
+HALF = VALUE_KEY_HEADS * ROWS
+ZS = 4
+SLOTS = 8 * ZS
+Z_ORDER = (1, 3, 2)
+
+
+def slot_of(core, place, z):
+    return (core * 4 + place) * ZS + z
+
+
+def copy_names():
+    names = [("z", r) for r in range(1, ZS)]
+    for kind in ("x", "y", "dx", "dy", "m0", "m1", "m2", "mk", "mv"):
+        names += [(kind, r) for r in range(ZS)]
+    return names
+
+
+NAMES = copy_names()
+
+
+def gather_attend(
+    block_rows, order_ref, q_ref, k_ref, v_ref, o_ref,
+    q_in, q_all, q_rest, own_rest, chunks, k_rest, v_rest, bias, q_sem, send_sem, recv_sem,
+):
+    ctx, z = lax.axis_index("ctx"), lax.axis_index("head")
+    bits = (lax.rem(ctx, 2), lax.rem(lax.div(ctx, 2), 2), lax.div(ctx, 4))
+    mate = (ctx + 1 - 2 * bits[0], z)
+    x_next = (ctx + 2 - 4 * bits[1], z)
+    y_next = (ctx + 4 - 8 * bits[2], z)
+    z_to = {r: (ctx, lax.rem(z + ZS - r, ZS)) for r in range(1, ZS)}
+
+    barrier = pltpu.get_barrier_semaphore()
+    partners = [mate, x_next, y_next] + [z_to[r] for r in range(1, ZS)]
+    for partner in partners:
+        pl.semaphore_signal(
+            barrier, inc=1, device_id=partner, device_id_type=pl.DeviceIdType.MESH
+        )
+    q_copy = pltpu.make_async_copy(q_ref, q_in, q_sem)
+    q_copy.start()
+
+    for which, ref in enumerate((k_ref, v_ref)):
+        base = which * HALF
+        for h in range(VALUE_KEY_HEADS):
+            lanes = slice(h * HEAD_DIMENSION, (h + 1) * HEAD_DIMENSION)
+            chunks[0, base + h * MAIN : base + (h + 1) * MAIN, :] = ref[0:MAIN, lanes]
+            own_rest[which, h * REST : (h + 1) * REST, :] = ref[MAIN:ROWS, lanes].astype(
+                jnp.float32
+            )
+        chunks[0, base + VALUE_KEY_HEADS * MAIN : base + HALF, :] = own_rest[which].astype(
+            jnp.bfloat16
+        )
+
+    ids = {name: number for number, name in enumerate(NAMES)}
+
+    def part(slot, half):
+        if half is None:
+            return chunks.at[slot]
+        return chunks.at[slot, half * HALF : (half + 1) * HALF]
+
+    def copy(name):
+        kind, r = name
+        target, source, sink, half = {
+            "z": (z_to.get(r), slot_of(0, 0, 0), slot_of(0, 0, r), None),
+            "x": (x_next, slot_of(0, 0, r), slot_of(0, 1, r), None),
+            "y": (y_next, slot_of(0, 0, r), slot_of(0, 2, r), None),
+            "dx": (x_next, slot_of(0, 2, r), slot_of(0, 3, r), 1),
+            "dy": (y_next, slot_of(0, 1, r), slot_of(0, 3, r), 0),
+            "m0": (mate, slot_of(0, 0, r), slot_of(1, 0, r), None),
+            "m1": (mate, slot_of(0, 1, r), slot_of(1, 1, r), None),
+            "m2": (mate, slot_of(0, 2, r), slot_of(1, 2, r), None),
+            "mk": (mate, slot_of(0, 3, r), slot_of(1, 3, r), 0),
+            "mv": (mate, slot_of(0, 3, r), slot_of(1, 3, r), 1),
+        }[kind]
+        return pltpu.make_async_remote_copy(
+            src_ref=part(source, half),
+            dst_ref=part(sink, half),
+            send_sem=send_sem.at[ids[name]],
+            recv_sem=recv_sem.at[ids[name]],
+            device_id=target,
+            device_id_type=pl.DeviceIdType.MESH,
+        )
+
+    copies = {name: copy(name) for name in NAMES}
+
+    def rest_rows(slot):
+        for which, sink in ((0, k_rest), (1, v_rest)):
+            top = which * HALF + VALUE_KEY_HEADS * MAIN
+            rows = chunks[slot, top : top + VALUE_KEY_HEADS * REST, :].astype(jnp.float32)
+            for h in range(VALUE_KEY_HEADS):
+                sink[h, slot * REST : (slot + 1) * REST, :] = rows[h * REST : (h + 1) * REST]
+
+    def arrived(*name):
+        copies[name].wait_recv()
+
+    def start(*name):
+        copies[name].start()
+
+    pl.semaphore_wait(barrier, len(partners))
+    for r in Z_ORDER:
+        start("z", r)
+    start("x", 0)
+    start("y", 0)
+    start("m0", 0)
+
+    lane = lax.broadcasted_iota(jnp.int32, (8, SLOTS * ROWS), 1)
+    late = lane >= SLOTS * MAIN
+    lane_slot = jnp.where(late, lax.div(lane - SLOTS * MAIN, REST), lax.div(lane, MAIN))
+    lane_token = jnp.where(late, MAIN + lax.rem(lane, REST), lax.rem(lane, MAIN))
+    key_pos = lane_token
+
+    def first_position(flips, r):
+        other = 0
+        for number, flip in enumerate(flips):
+            bit = 1 - bits[number] if flip else bits[number]
+            other = other + bit * (1 << number)
+        row = (other * ZS + lax.rem(z + r, ZS)) * ROWS
+        return order_ref[lax.div(row, block_rows)] * block_rows + lax.rem(row, block_rows)
+
+    for core in range(2):
+        for place in range(4):
+            for r in range(ZS):
+                at = first_position((core, place % 2, place // 2), r)
+                key_pos = key_pos + jnp.where(lane_slot == slot_of(core, place, r), at, 0)
+    row = lax.broadcasted_iota(jnp.int32, (HALF, SLOTS * ROWS), 0)
+    row_token = jnp.where(row >= GROUP * MAIN, MAIN + lax.rem(row, REST), lax.rem(row, MAIN))
+    visible = key_pos[0:1, :] - first_position((0, 0, 0), 0) <= row_token
+    bias[...] = jnp.where(visible, 0.0, -jnp.inf)
+
+    q_copy.wait()
+    for h in range(VALUE_KEY_HEADS):
+        for g in range(GROUP):
+            lanes = slice((h * GROUP + g) * HEAD_DIMENSION, (h * GROUP + g + 1) * HEAD_DIMENSION)
+            q_all[h, g * MAIN : (g + 1) * MAIN, :] = q_in[0:MAIN, lanes]
+            q_rest[h, g * REST : (g + 1) * REST, :] = q_in[MAIN:ROWS, lanes].astype(jnp.float32)
+        q_all[h, GROUP * MAIN : HALF, :] = q_rest[h].astype(jnp.bfloat16)
+    rest_rows(0)
+
+    def pass_first(r):
+        arrived("z", r)
+        start("x", r)
+        start("y", r)
+        start("m0", r)
+        rest_rows(slot_of(0, 0, r))
+
+    def pass_second(r):
+        arrived("x", r)
+        start("dy", r)
+        start("m1", r)
+        arrived("y", r)
+        start("dx", r)
+        start("m2", r)
+        rest_rows(slot_of(0, 1, r))
+        rest_rows(slot_of(0, 2, r))
+
+    def pass_third(r):
+        arrived("dy", r)
+        start("mk", r)
+        arrived("dx", r)
+        start("mv", r)
+        rest_rows(slot_of(0, 3, r))
+        for place in range(3):
+            arrived("m%d" % place, r)
+            rest_rows(slot_of(1, place, r))
+
+    pass_second(0)
+    for r in Z_ORDER:
+        pass_first(r)
+    pass_third(0)
+    for r in Z_ORDER:
+        pass_second(r)
+    for r in Z_ORDER:
+        pass_third(r)
+    for r in (0,) + Z_ORDER:
+        arrived("mk", r)
+        arrived("mv", r)
+        rest_rows(slot_of(1, 3, r))
+
+    scale = HEAD_DIMENSION ** (-0.5)
+    whole = (((1,), (1,)), ((), ()))
+    for h in range(VALUE_KEY_HEADS):
+        rows = slice(h * MAIN, (h + 1) * MAIN)
+        queries = q_all[h]
+        keys = chunks[:, rows, :].reshape(SLOTS * MAIN, HEAD_DIMENSION)
+        values = chunks[:, HALF + h * MAIN : HALF + (h + 1) * MAIN, :].reshape(
+            SLOTS * MAIN, HEAD_DIMENSION
+        )
+        scores = jnp.concatenate(
+            [
+                lax.dot_general(queries, keys, whole, preferred_element_type=jnp.float32),
+                lax.dot_general(
+                    queries,
+                    k_rest[h].astype(jnp.bfloat16),
+                    whole,
+                    preferred_element_type=jnp.float32,
+                ),
+            ],
+            axis=1,
+        ) + bias[...]
+        top = jnp.max(scores, axis=1, keepdims=True)
+        weights = jnp.exp((scores - top) * scale)
+        total = jnp.sum(weights, axis=1, keepdims=True)
+        weights = weights.astype(jnp.bfloat16)
+        mixed = jnp.dot(
+            weights[:, : SLOTS * MAIN], values, preferred_element_type=jnp.float32
+        ) + jnp.dot(
+            weights[:, SLOTS * MAIN :],
+            v_rest[h].astype(jnp.bfloat16),
+            preferred_element_type=jnp.float32,
+        )
+        mixed = mixed / total
+        for g in range(GROUP):
+            lanes = slice((h * GROUP + g) * HEAD_DIMENSION, (h * GROUP + g + 1) * HEAD_DIMENSION)
+            o_ref[0:MAIN, lanes] = mixed[g * MAIN : (g + 1) * MAIN].astype(jnp.bfloat16)
+            first = GROUP * MAIN + g * REST
+            o_ref[MAIN:ROWS, lanes] = mixed[first : first + REST].astype(jnp.bfloat16)
+
+    for name in NAMES:
+        copies[name].wait_send()
+
+
+def on_device_gathered(queries, keys, values, block_order):
+    block_rows = queries.shape[0] * lax.axis_size("ctx") * lax.axis_size("head")
+    block_rows = block_rows // block_order.shape[0]
+    bf16, f32 = jnp.bfloat16, jnp.float32
+    in_vmem = pl.BlockSpec(memory_space=pltpu.VMEM)
+    return pl.pallas_call(
+        functools.partial(gather_attend, block_rows),
+        out_shape=jax.ShapeDtypeStruct(queries.shape, bf16),
+        in_specs=[
+            pl.BlockSpec(memory_space=pltpu.SMEM),
+            pl.BlockSpec(memory_space=pl.ANY),
+            in_vmem,
+            in_vmem,
+        ],
+        out_specs=in_vmem,
+        scratch_shapes=[
+            pltpu.VMEM(queries.shape, bf16),
+            pltpu.VMEM((VALUE_KEY_HEADS, HALF, HEAD_DIMENSION), bf16),
+            pltpu.VMEM((VALUE_KEY_HEADS, GROUP * REST, HEAD_DIMENSION), f32),
+            pltpu.VMEM((2, VALUE_KEY_HEADS * REST, HEAD_DIMENSION), f32),
+            pltpu.VMEM((SLOTS, 2 * HALF, HEAD_DIMENSION), bf16),
+            pltpu.VMEM((VALUE_KEY_HEADS, SLOTS * REST, HEAD_DIMENSION), f32),
+            pltpu.VMEM((VALUE_KEY_HEADS, SLOTS * REST, HEAD_DIMENSION), f32),
+            pltpu.VMEM((HALF, SLOTS * ROWS), f32),
+            pltpu.SemaphoreType.DMA,
+            pltpu.SemaphoreType.DMA((len(NAMES),)),
+            pltpu.SemaphoreType.DMA((len(NAMES),)),
+        ],
+        compiler_params=pltpu.CompilerParams(
+            collective_id=0, has_side_effects=True, vmem_limit_bytes=32 * 1024 * 1024
+        ),
+    )(block_order, queries, keys, values)
+
+
+def gathers_whole(mesh, queries, block_order):
+    if mesh.shape["ctx"] != 8 or mesh.shape["head"] != ZS:
+        return False
+    rows = queries.shape[0]
+    return rows == SLOTS * ROWS and (rows // block_order.shape[0]) % ROWS == 0
+
+
 def solution(mesh):
     placed = (P(("ctx", "head"), None), P(("ctx", "head"), None), P(("ctx", "head"), None), P())
-    return jax.shard_map(
-        on_device, mesh=mesh, in_specs=placed, out_specs=P(("ctx", "head"), None), check_vma=False
-    )
+
+    def run(queries, keys, values, block_order):
+        body = on_device_gathered if gathers_whole(mesh, queries, block_order) else on_device
+        return jax.shard_map(
+            body, mesh=mesh, in_specs=placed, out_specs=P(("ctx", "head"), None), check_vma=False
+        )(queries, keys, values, block_order)
+
+    return run

time: 80.1 us -> 30.7 us (0.38)
  the two profiles are of different devices: /device:TPU:0 before, /device:TPU:1 now
where the time goes in v1:
time: 30.7 us; the launch traced here: 30.4 us
  Pallas kernels  26.4 us (86%)
  local copies, waits for them, and re-layouts  3.99 us (13%)
    pallas_call x1, Pallas kernels, on_device_gathered(): pl.pallas_call(functools.partial(gather_attend, block_rows), out_shape=ja...  26.4 us
    unnamed x9, local copies, waits for them, and re-layouts  3.99 us

profile of v1, /device:TPU:1, one launch (start us, length us, event | category | flops | bytes accessed | tf_op | source)
XLA Modules:
  0.0 30.4 jit_solution(1298848195193488129)
XLA Ops:
  0.0 0.0 copy-start
  0.0 1.0 %copy-done = bf16[20,8192]{1,0:T(8,128)(2,1)S(1)} copy-done((bf16[20,8192]{1,0:T(8,128)(2,1)S(1)}, bf16[20,8192]{1,0:T(8,128)(2,1)}, u32[]{:S(2)}) %copy-start) | copy-done | bytes 327704
  1.0 0.0 copy-start.1
  1.0 0.8 %copy-done.1 = bf16[20,1024]{1,0:T(8,128)(2,1)S(1)} copy-done((bf16[20,1024]{1,0:T(8,128)(2,1)S(1)}, bf16[20,1024]{1,0:T(8,128)(2,1)}, u32[]{:S(2)}) %copy-start.1) | copy-done | bytes 40984
  1.8 0.0 copy-start.2
  1.8 0.8 %copy-done.2 = bf16[20,1024]{1,0:T(8,128)(2,1)S(1)} copy-done((bf16[20,1024]{1,0:T(8,128)(2,1)S(1)}, bf16[20,1024]{1,0:T(8,128)(2,1)}, u32[]{:S(2)}) %copy-start.2) | copy-done | bytes 40984
  2.6 0.0 copy-start.3
  2.6 0.7 %copy-done.3 = s32[16]{0:T(128)S(1)} copy-done((s32[16]{0:T(128)S(1)}, s32[16]{0:T(128)}, u32[]{:S(2)}) %copy-start.3) | copy-done | bytes 88
  3.3 26.4 %shard_map.46 = bf16[20,8192]{1,0:T(8,128)(2,1)S(1)} custom-call(s32[16]{0:T(128)S(1)} %copy-done.3, bf16[20,8192]{1,0:T(8,128)(2,1)S(1)} %copy-done, bf16[20,1024]{1,0:T(8,128)(2,1)S(1)} %copy-done.1, bf16[20,1024]{1,0:T(8,128)(2,1)S(1)} %copy-done.2), custom_call_target="tpu_custom_call" | custom-call | tf_op jit(solution)/shard_map/pallas_call | solution.py:407
  29.6 0.7 %copy.6 = bf16[20,8192]{1,0:T(8,128)(2,1)} copy(bf16[20,8192]{1,0:T(8,128)(2,1)S(1)} %shard_map.46) | data formatting | bytes 655360
Async XLA Ops:
  0.0 1.0 %copy-start = (bf16[20,8192]{1,0:T(8,128)(2,1)S(1)}, bf16[20,8192]{1,0:T(8,128)(2,1)}, u32[]{:S(2)}) copy-start(bf16[20,8192]{1,0:T(8,128)(2,1)} %q_ref.1) | copy-start | bytes 983044
  1.0 0.8 %copy-start.1 = (bf16[20,1024]{1,0:T(8,128)(2,1)S(1)}, bf16[20,1024]{1,0:T(8,128)(2,1)}, u32[]{:S(2)}) copy-start(bf16[20,1024]{1,0:T(8,128)(2,1)} %k_ref.1) | copy-start | bytes 122884
  1.8 0.8 %copy-start.2 = (bf16[20,1024]{1,0:T(8,128)(2,1)S(1)}, bf16[20,1024]{1,0:T(8,128)(2,1)}, u32[]{:S(2)}) copy-start(bf16[20,1024]{1,0:T(8,128)(2,1)} %v_ref.1) | copy-start | bytes 122884
  2.6 0.7 %copy-start.3 = (s32[16]{0:T(128)S(1)}, s32[16]{0:T(128)}, u32[]{:S(2)}) copy-start(s32[16]{0:T(128)} %order_ref.1) | copy-start | bytes 196

commit v2 on v1

--- a/solution.py
+++ b/solution.py
@@ -200,8 +200,9 @@
 
 
 def gather_attend(
-    block_rows, order_ref, q_ref, k_ref, v_ref, o_ref,
-    q_in, q_all, q_rest, own_rest, chunks, k_rest, v_rest, bias, q_sem, send_sem, recv_sem,
+    block_rows, order_hbm, q_hbm, k_hbm, v_hbm, o_ref,
+    order_ref, k_ref, v_ref, q_in, q_all, q_rest, own_rest, chunks, k_rest, v_rest, bias,
+    in_sem, send_sem, recv_sem,
 ):
     ctx, z = lax.axis_index("ctx"), lax.axis_index("head")
     bits = (lax.rem(ctx, 2), lax.rem(lax.div(ctx, 2), 2), lax.div(ctx, 4))
@@ -210,16 +211,24 @@
     y_next = (ctx + 4 - 8 * bits[2], z)
     z_to = {r: (ctx, lax.rem(z + ZS - r, ZS)) for r in range(1, ZS)}
 
+    loads = [
+        pltpu.make_async_copy(source, sink, in_sem.at[number])
+        for number, (source, sink) in enumerate(
+            ((k_hbm, k_ref), (v_hbm, v_ref), (order_hbm, order_ref), (q_hbm, q_in))
+        )
+    ]
+    for load in loads:
+        load.start()
+
     barrier = pltpu.get_barrier_semaphore()
     partners = [mate, x_next, y_next] + [z_to[r] for r in range(1, ZS)]
     for partner in partners:
         pl.semaphore_signal(
             barrier, inc=1, device_id=partner, device_id_type=pl.DeviceIdType.MESH
         )
-    q_copy = pltpu.make_async_copy(q_ref, q_in, q_sem)
-    q_copy.start()
 
     for which, ref in enumerate((k_ref, v_ref)):
+        loads[which].wait()
         base = which * HALF
         for h in range(VALUE_KEY_HEADS):
             lanes = slice(h * HEAD_DIMENSION, (h + 1) * HEAD_DIMENSION)
@@ -283,6 +292,7 @@
     start("y", 0)
     start("m0", 0)
 
+    loads[2].wait()
     lane = lax.broadcasted_iota(jnp.int32, (8, SLOTS * ROWS), 1)
     late = lane >= SLOTS * MAIN
     lane_slot = jnp.where(late, lax.div(lane - SLOTS * MAIN, REST), lax.div(lane, MAIN))
@@ -307,7 +317,7 @@
     visible = key_pos[0:1, :] - first_position((0, 0, 0), 0) <= row_token
     bias[...] = jnp.where(visible, 0.0, -jnp.inf)
 
-    q_copy.wait()
+    loads[3].wait()
     for h in range(VALUE_KEY_HEADS):
         for g in range(GROUP):
             lanes = slice((h * GROUP + g) * HEAD_DIMENSION, (h * GROUP + g + 1) * HEAD_DIMENSION)
@@ -403,18 +413,16 @@
     block_rows = queries.shape[0] * lax.axis_size("ctx") * lax.axis_size("head")
     block_rows = block_rows // block_order.shape[0]
     bf16, f32 = jnp.bfloat16, jnp.float32
-    in_vmem = pl.BlockSpec(memory_space=pltpu.VMEM)
+    in_hbm = pl.BlockSpec(memory_space=pltpu.HBM)
     return pl.pallas_call(
         functools.partial(gather_attend, block_rows),
         out_shape=jax.ShapeDtypeStruct(queries.shape, bf16),
-        in_specs=[
-            pl.BlockSpec(memory_space=pltpu.SMEM),
-            pl.BlockSpec(memory_space=pl.ANY),
-            in_vmem,
-            in_vmem,
-        ],
-        out_specs=in_vmem,
+        in_specs=[in_hbm] * 4,
+        out_specs=pl.BlockSpec(memory_space=pltpu.VMEM),
         scratch_shapes=[
+            pltpu.SMEM(block_order.shape, jnp.int32),
+            pltpu.VMEM(keys.shape, bf16),
+            pltpu.VMEM(values.shape, bf16),
             pltpu.VMEM(queries.shape, bf16),
             pltpu.VMEM((VALUE_KEY_HEADS, HALF, HEAD_DIMENSION), bf16),
             pltpu.VMEM((VALUE_KEY_HEADS, GROUP * REST, HEAD_DIMENSION), f32),
@@ -423,12 +431,12 @@
             pltpu.VMEM((VALUE_KEY_HEADS, SLOTS * REST, HEAD_DIMENSION), f32),
             pltpu.VMEM((VALUE_KEY_HEADS, SLOTS * REST, HEAD_DIMENSION), f32),
             pltpu.VMEM((HALF, SLOTS * ROWS), f32),
-            pltpu.SemaphoreType.DMA,
+            pltpu.SemaphoreType.DMA((4,)),
             pltpu.SemaphoreType.DMA((len(NAMES),)),
             pltpu.SemaphoreType.DMA((len(NAMES),)),
         ],
         compiler_params=pltpu.CompilerParams(
-            collective_id=0, has_side_effects=True, vmem_limit_bytes=32 * 1024 * 1024
+            collective_id=0, has_side_effects=True, vmem_limit_bytes=60 * 1024 * 1024
         ),
     )(block_order, queries, keys, values)
 

time: 30.7 us -> 28 us (0.912)
  local copies, waits for them, and re-layouts: 3.99 us -> 1.77 us
    unnamed x9 -> x1, local copies, waits for them, and re-layouts: 3.99 us -> 1.77 us
where the time goes in v2:
time: 28 us; the launch traced here: 27.9 us
  Pallas kernels  26.1 us (93%)
  local copies, waits for them, and re-layouts  1.77 us (6%)
    pallas_call x1, Pallas kernels, on_device_gathered(): pl.pallas_call(functools.partial(gather_attend, block_rows), out_shape=ja...  26.1 us
    unnamed x1, local copies, waits for them, and re-layouts  1.77 us

profile of v2, /device:TPU:1, one launch (start us, length us, event | category | flops | bytes accessed | tf_op | source)
XLA Modules:
  0.0 27.9 jit_solution(11210864714287064208)
XLA Ops:
  0.0 26.1 %shard_map.46 = bf16[20,8192]{1,0:T(8,128)(2,1)} custom-call(s32[16]{0:T(128)} %order_hbm.1, bf16[20,8192]{1,0:T(8,128)(2,1)} %q_hbm.1, bf16[20,1024]{1,0:T(8,128)(2,1)} %k_hbm.1, bf16[20,1024]{1,0:T(8,128)(2,1)} %v_hbm.1), custom_call_target="tpu_custom_call" | custom-call | tf_op jit(solution)/shard_map/pallas_call | solution.py:417
  26.1 1.8 %copy.6 = bf16[20,8192]{1,0:T(8,128)(2,1)} copy(bf16[20,8192]{1,0:T(8,128)(2,1)} %shard_map.46) | data formatting | bytes 655360

commit v3 on v2

--- a/solution.py
+++ b/solution.py
@@ -183,6 +183,7 @@
 ZS = 4
 SLOTS = 8 * ZS
 Z_ORDER = (1, 3, 2)
+DIRECT = (0, 2)
 
 
 def slot_of(core, place, z):
@@ -209,6 +210,7 @@
     mate = (ctx + 1 - 2 * bits[0], z)
     x_next = (ctx + 2 - 4 * bits[1], z)
     y_next = (ctx + 4 - 8 * bits[2], z)
+    across = (ctx + 6 - 4 * bits[1] - 8 * bits[2], z)
     z_to = {r: (ctx, lax.rem(z + ZS - r, ZS)) for r in range(1, ZS)}
 
     loads = [
@@ -221,7 +223,7 @@
         load.start()
 
     barrier = pltpu.get_barrier_semaphore()
-    partners = [mate, x_next, y_next] + [z_to[r] for r in range(1, ZS)]
+    partners = [mate, x_next, y_next, across] + [z_to[r] for r in range(1, ZS)]
     for partner in partners:
         pl.semaphore_signal(
             barrier, inc=1, device_id=partner, device_id_type=pl.DeviceIdType.MESH
@@ -249,12 +251,13 @@
 
     def copy(name):
         kind, r = name
+        direct = r in DIRECT
         target, source, sink, half = {
             "z": (z_to.get(r), slot_of(0, 0, 0), slot_of(0, 0, r), None),
             "x": (x_next, slot_of(0, 0, r), slot_of(0, 1, r), None),
             "y": (y_next, slot_of(0, 0, r), slot_of(0, 2, r), None),
-            "dx": (x_next, slot_of(0, 2, r), slot_of(0, 3, r), 1),
-            "dy": (y_next, slot_of(0, 1, r), slot_of(0, 3, r), 0),
+            "dx": (across if direct else x_next, slot_of(0, 0 if direct else 2, r), slot_of(0, 3, r), 1),
+            "dy": (across if direct else y_next, slot_of(0, 0 if direct else 1, r), slot_of(0, 3, r), 0),
             "m0": (mate, slot_of(0, 0, r), slot_of(1, 0, r), None),
             "m1": (mate, slot_of(0, 1, r), slot_of(1, 1, r), None),
             "m2": (mate, slot_of(0, 2, r), slot_of(1, 2, r), None),
@@ -291,6 +294,9 @@
     start("x", 0)
     start("y", 0)
     start("m0", 0)
+    if 0 in DIRECT:
+        start("dy", 0)
+        start("dx", 0)
 
     loads[2].wait()
     lane = lax.broadcasted_iota(jnp.int32, (8, SLOTS * ROWS), 1)
@@ -331,14 +337,19 @@
         start("x", r)
         start("y", r)
         start("m0", r)
+        if r in DIRECT:
+            start("dy", r)
+            start("dx", r)
         rest_rows(slot_of(0, 0, r))
 
     def pass_second(r):
         arrived("x", r)
-        start("dy", r)
+        if r not in DIRECT:
+            start("dy", r)
         start("m1", r)
         arrived("y", r)
-        start("dx", r)
+        if r not in DIRECT:
+            start("dx", r)
         start("m2", r)
         rest_rows(slot_of(0, 1, r))
         rest_rows(slot_of(0, 2, r))

time: 28 us -> 27.7 us (0.989)
  Pallas kernels: 26.1 us -> 25.7 us
    pallas_call x1, Pallas kernels: 26.1 us -> 25.7 us  [on_device_gathered(): pl.pallas_call(functools.partial(gather_attend, block_rows), out_shape=ja...]
where the time goes in v3:
time: 27.7 us; the launch traced here: 27.5 us
  Pallas kernels  25.7 us (93%)
  local copies, waits for them, and re-layouts  1.77 us (6%)
    pallas_call x1, Pallas kernels, on_device_gathered(): pl.pallas_call(functools.partial(gather_attend, block_rows), out_shape=ja...  25.7 us
    unnamed x1, local copies, waits for them, and re-layouts  1.77 us

profile of v3, /device:TPU:1, one launch (start us, length us, event | category | flops | bytes accessed | tf_op | source)
XLA Modules:
  0.0 27.5 jit_solution(11907807628376690608)
XLA Ops:
  0.0 25.7 %shard_map.46 = bf16[20,8192]{1,0:T(8,128)(2,1)} custom-call(s32[16]{0:T(128)} %order_hbm.1, bf16[20,8192]{1,0:T(8,128)(2,1)} %q_hbm.1, bf16[20,1024]{1,0:T(8,128)(2,1)} %k_hbm.1, bf16[20,1024]{1,0:T(8,128)(2,1)} %v_hbm.1), custom_call_target="tpu_custom_call" | custom-call | tf_op jit(solution)/shard_map/pallas_call | solution.py:428
  25.7 1.8 %copy.6 = bf16[20,8192]{1,0:T(8,128)(2,1)} copy(bf16[20,8192]{1,0:T(8,128)(2,1)} %shard_map.46) | data formatting | bytes 655360
